TPU v7x, 32 devices: a whole 2x2x4 slice. The times are simulated.
32 devices in a mesh: rows: 32 (over z, y, x, core).
Axes of the slice: x: 2, y: 2, z: 4, core: 2. Of those that a mesh axis runs over, the one named last changes fastest.
Arguments:
- trailing: float32 [16384, 1024], P('rows'), may hold values from -50 to 50
- leaf_vectors: float32 [16384, 256], P('rows'), may hold values from -2 to 2, as said below
- leaf_factors: float32 [8192, 256], P('rows'), may hold values from -2 to 2, as said below
- tree_vectors: float32 [8192, 256], P('rows'), may hold values from -2 to 2, as said below
- tree_factors: float32 [8192, 256], P('rows'), may hold values from -2 to 2, as said below
- inverse_factor: float32 [256, 256], replicated, may hold values from -2 to 2, as said below
Outputs:
- updated: float32 [16384, 1024], P('rows')
- panel_basis: float32 [16384, 256], P('rows')
- panel_gram: float32 [256, 256], replicated
Inputs may be any that keep to these rules, and one draw needn't show every extreme that they name: Within each leaf, rows 0 to 255 of leaf_vectors form a unit lower triangular matrix (ones on the diagonal, zeros above); leaf_factors_p is the upper triangular factor for which I - leaf_vectors_p leaf_factors_p leaf_vectors_p^T is orthogonal. `leaf_factors`: each block is upper triangular and is the factor described for leaf_vectors. `tree_vectors`: each block is upper triangular, diagonal included; with Y = [I; tree_vectors_q], I - Y tree_factors_q Y^T is orthogonal. `tree_factors`: each block is upper triangular and is the factor described for tree_vectors. `inverse_factor`: upper triangular with a positive diagonal.
All inputs are finite; a program needn't handle non-finite values.
Results may differ from a plain program's by a relative error of at most 0.00018.
Values sent between devices are 32-bit elements; how exact they have to be, the bound alone decides.
No kernel may reach another device: no remote copies, remote signals or barrier semaphores. Data moves between devices by JAX's collectives and lax.ppermute only.
A program may use at most 64 MiB of HBM per device.

v0:
```python
import functools
import jax
import jax.numpy as jnp
from jax import lax
from jax.experimental import pallas as pl
from jax.experimental.pallas import tpu as pltpu
from jax.sharding import PartitionSpec as P

F32 = jnp.float32
BF16 = jnp.bfloat16
EXTRA = 8
PARAMS = pltpu.CompilerParams(vmem_limit_bytes=20 * 1024 * 1024)
WHOLE = pl.BlockSpec(memory_space=pltpu.VMEM)
SCALAR = pl.BlockSpec(memory_space=pltpu.SMEM)
AWAY = pl.BlockSpec(memory_space=pltpu.HBM)


def halves(value):
    high = value.astype(BF16)
    return high, (value - high.astype(F32)).astype(BF16)


def times(left, right, sides):
    first = jnp.concatenate([left[0], left[0], left[1]], axis=sides[0])
    second = jnp.concatenate([right[0], right[1], right[0]], axis=sides[1])
    dims = ((sides[:1], sides[1:]), ((), ()))
    return lax.dot_general(first, second, dims, preferred_element_type=F32)


def plain(left, right):
    return times(left, right, (1, 0))


def by_transpose(left, right):
    return times(left, right, (1, 1))


def masks(size):
    row = lax.broadcasted_iota(jnp.int32, (size, size), 0)
    col = lax.broadcasted_iota(jnp.int32, (size, size), 1)
    return row, col


def diagonal_of(square):
    row, col = masks(square.shape[0])
    return jnp.sum(jnp.where(row == col, square, 0.0), axis=0, keepdims=True)


def pack_kernel(me_ref, *refs):
    sources, (low_ref, high_ref, part_ref), (buffer_ref, sems) = refs[:4], refs[4:7], refs[7:]
    copies = [pltpu.make_async_copy(source, buffer_ref.at[i], sems.at[i]) for i, source in enumerate(sources)]
    for copy in copies:
        copy.start()
    for copy in copies:
        copy.wait()
    core = me_ref[0] % 2
    half = buffer_ref.shape[1] // 2
    row, col = masks(half)
    both_vectors = by_core(core, buffer_ref[0], buffer_ref[2])
    both_factors = by_core(core, buffer_ref[1], buffer_ref[3])
    for vectors, factors, out_ref in zip(both_vectors, both_factors, (low_ref, high_ref)):
        first, second = factors[:half, :half], factors[half:, half:]
        square = jnp.where(row > col, first.T, jnp.where(row < col, second, 0.0))
        t_rows = jnp.concatenate([square, factors[:half, half:].T], axis=1)
        t_diagonal = jnp.concatenate([diagonal_of(first), diagonal_of(second)], axis=1)
        first, second = vectors[:half, :half], vectors[half:, half:]
        square = jnp.where(row <= col, first, second.T)
        v_rows = jnp.concatenate([square, vectors[:half, half:]], axis=1)
        v_diagonal = jnp.concatenate([diagonal_of(second)] * 2, axis=1)
        line = lax.broadcasted_iota(jnp.int32, (EXTRA, 2 * half), 0)
        diagonals = jnp.where(line == 0, t_diagonal, v_diagonal)
        for part in range(2):
            rows = slice(part * half // 2, (part + 1) * half // 2)
            out_ref[part, : half // 2] = t_rows[rows]
            out_ref[part, half // 2 : half // 2 + EXTRA] = diagonals
            out_ref[part, half // 2 + EXTRA :] = v_rows[rows]
    part_ref[...] = low_ref[core]


def unpack_factors(first, second):
    half = first.shape[1] // 2
    rows = jnp.concatenate([first[: half // 2], second[: half // 2]], axis=0)
    row, col = masks(half)
    square, corner = rows[:, :half], rows[:, half:]
    diagonal = first[half // 2 : half // 2 + 1]
    upper_left = jnp.where(row > col, square, jnp.where(row == col, diagonal[:, :half], 0.0))
    lower_right = jnp.where(row > col, square.T, jnp.where(row == col, diagonal[:, half:], 0.0))
    above = jnp.concatenate([upper_left, jnp.zeros_like(upper_left)], axis=1)
    return halves(jnp.concatenate([above, jnp.concatenate([corner, lower_right], axis=1)], axis=0))


def unpack_vectors(first, second):
    half = first.shape[1] // 2
    start = half // 2 + EXTRA
    rows = jnp.concatenate([first[start:], second[start:]], axis=0)
    row, col = masks(half)
    square, corner = rows[:, :half], rows[:, half:]
    diagonal = first[half // 2 + 1 : half // 2 + 2, :half]
    upper_left = jnp.where(row <= col, square, 0.0)
    lower_right = jnp.where(row < col, square.T, jnp.where(row == col, diagonal, 0.0))
    above = jnp.concatenate([upper_left, corner], axis=1)
    return halves(jnp.concatenate([above, jnp.concatenate([jnp.zeros_like(corner), lower_right], axis=1)], axis=0))


def unpack(first, second):
    return unpack_vectors(first, second), unpack_factors(first, second)


def by_core(core, mine, there):
    odd = core == 1
    return jnp.where(odd, there, mine), jnp.where(odd, mine, there)


def place(me):
    return (me >> 1) & 3


def by_place(me, parts, wanted):
    source = place(me) ^ wanted
    out = parts[0]
    for r in range(1, 4):
        out = jnp.where(source == r, parts[r], out)
    return out


def tree_node(low, high, reflector):
    vectors, factors = reflector
    node = by_transpose(halves(low + plain(halves(high), vectors)), factors)
    return low - node, high - by_transpose(halves(node), vectors)


def leaf_first_kernel(
    me_ref, trailing_hbm, vectors_hbm, factors_hbm, inverse_hbm,
    own_ref, away_one, away_two, rest_ref, later_ref, inverse_ref, across_ref, combined_ref,
    part_ref, vectors_ref, factors_ref, value_ref, away_ref, sems,
):
    count, rows, width = part_ref.shape
    copies = []

    def fetch(source, target):
        copies.append(pltpu.make_async_copy(source, target, sems.at[len(copies)]))
        copies[-1].start()
        return copies[-1]

    def fetch_part(b, target):
        cuts = [slice(c, c + width) for c in range(0, rows, width)]
        return [fetch(trailing_hbm.at[c, pl.ds(b * width, width)], target.at[c]) for c in cuts]

    first = [fetch(vectors_hbm, vectors_ref), fetch(factors_hbm, factors_ref)]
    parts = [fetch_part(b, part_ref.at[b]) for b in range(count)]
    for copy in first:
        copy.wait()
    last = [fetch_part(count + b, later_ref.at[b]) for b in range(later_ref.shape[0])]
    last.append([fetch(inverse_hbm, inverse_ref)])
    vectors = vectors_ref[...]
    across = halves(vectors.T)
    across_ref[0], across_ref[1] = across
    combined = halves(by_transpose(halves(vectors), halves(factors_ref[...])))
    combined_ref[0], combined_ref[1] = combined
    for b in range(count):
        for copy in parts[b]:
            copy.wait()
        leaf_block(me_ref, part_ref[b], across, combined, value_ref, rest_ref.at[b], own_ref, away_ref, b)
    panel = part_ref[0]
    value_ref[...] = plain(halves(panel.T), halves(panel))
    hand_over(me_ref, value_ref, own_ref, away_ref, count)
    cut = away_one.shape[0]
    away_one[...] = away_ref[:cut]
    away_two[...] = away_ref[cut:]
    for group in last:
        for copy in group:
            copy.wait()


def hand_over(me_ref, value_ref, own_ref, away_ref, slot):
    half = value_ref.shape[0] // 2
    core = me_ref[0] % 2
    target = slice(slot * half, (slot + 1) * half)
    own_ref[target] = value_ref[pl.ds(pl.multiple_of(core * half, half), half)]
    away_ref[target] = value_ref[pl.ds(pl.multiple_of((1 - core) * half, half), half)]


def leaf_block(me_ref, part, across, combined, value_ref, rest_ref, own_ref, away_ref, slot):
    width = value_ref.shape[0]
    out = part - plain(combined, halves(plain(across, halves(part))))
    rest_ref[...] = out[width:]
    value_ref[...] = out[:width].T
    hand_over(me_ref, value_ref, own_ref, away_ref, slot)


def leaf_second_kernel(me_ref, later_ref, across_ref, combined_ref, own_ref, rest_ref, *refs):
    aways, value_ref = refs[:-1], refs[-1]
    half = value_ref.shape[0] // 2
    across = across_ref[0], across_ref[1]
    combined = combined_ref[0], combined_ref[1]
    for b in range(later_ref.shape[0]):
        own_b = own_ref.at[pl.ds(b * half, half)]
        leaf_block(me_ref, later_ref[b], across, combined, value_ref, rest_ref.at[b], own_b, aways[b], 0)


def store_kernel(me_ref, first_ref, second_ref, inverse_ref, mark_ref, updated_hbm, basis_hbm, basis_ref, sems):
    count, width = first_ref.shape[:2]
    copies = []
    for b in range(count + second_ref.shape[0]):
        source = first_ref.at[b] if b < count else second_ref.at[b - count]
        target = updated_hbm.at[pl.ds(width, width), pl.ds(b * width, width)]
        copies.append(pltpu.make_async_copy(source, target, sems.at[b]))
        copies[-1].start()
    basis_ref[...] = plain(halves(first_ref[0]), halves(inverse_ref[...]))
    copies.append(pltpu.make_async_copy(basis_ref, basis_hbm.at[pl.ds(width, width)], sems.at[len(copies)]))
    mark_ref[...] = jnp.zeros_like(mark_ref)
    copies[-1].start()
    for copy in copies:
        copy.wait()


def core_kernel(
    me_ref, own_a_ref, own_b_ref, one_ref, two_ref, *refs
):
    more = len(refs) - 12
    there_bs, packed_ref = refs[:more], refs[more]
    sends, dones, (gram_ref, low_ref, high_ref) = refs[more + 1 : more + 5], refs[more + 5 : more + 9], refs[more + 9 :]
    me = me_ref[0]
    width = own_a_ref.shape[1]
    half = width // 2
    quarter = half // 4
    cut = own_a_ref.shape[0] - half
    count = cut // half + len(there_bs)
    odd = me % 2 == 1
    there_a = jnp.concatenate([one_ref[...], two_ref[...]], axis=0)
    gram_ref[...] = own_a_ref[cut:] + there_a[cut:]
    mine = jnp.concatenate([own_a_ref[:cut], own_b_ref[...]], axis=0)
    there = jnp.concatenate([there_a[:cut]] + [ref[...] for ref in there_bs], axis=0)
    low = jnp.where(odd, there, mine)
    high = jnp.where(odd, mine, there)
    low, high = tree_node(low, high, unpack(packed_ref[0], packed_ref[1]))
    low_ref[...] = low
    high_ref[...] = high
    for r in range(4):
        start = (place(me) ^ r) * quarter
        for b in range(count):
            source = pl.ds(pl.multiple_of(b * half + start, quarter), quarter)
            target = slice(b * quarter, (b + 1) * quarter)
            sends[r][target] = low_ref[source]
            dones[r][target] = high_ref[source]
        if sends[r].shape[0] > count * quarter:
            sends[r][count * quarter :] = jnp.zeros_like(sends[r][count * quarter :])


def gather_kernel(me_ref, *refs):
    parts, (stack_ref, held_ref) = refs[:4], refs[4:]
    for r in range(1, 4):
        stack_ref[r - 1] = parts[r][...]
    held_ref[...] = by_place(me_ref[0], [ref[...] for ref in parts], 0)


def hold_kernel(me_ref, held_ref, part_ref, out_ref, *, level):
    rows = slice(0, out_ref.shape[0])
    out_ref[...] = jnp.where((me_ref[0] >> level) % 2 == 1, part_ref[rows], held_ref[rows])


def add_kernel(me_ref, first_ref, second_ref, out_ref):
    out_ref[...] = first_ref[...] + second_ref[...]


def fill(send_ref, value):
    cols = value.shape[0]
    send_ref[:cols] = value
    if send_ref.shape[0] > cols:
        send_ref[cols:] = jnp.zeros_like(send_ref[cols:])


def prepare_kernel(me_ref, packed_ref, stack_ref, stack_there_ref, joint_ref, vectors_ref, held_ref):
    me = me_ref[0]
    pairs = [(packed_ref[0], packed_ref[1])]
    pairs += [by_core(me % 2, stack_ref[r], stack_there_ref[r]) for r in range(3)]
    firsts, seconds = [pair[0] for pair in pairs], [pair[1] for pair in pairs]
    pairs = [(by_place(me, firsts, j), by_place(me, seconds, j)) for j in range(4)]
    held_ref[0], held_ref[1] = pairs[0]
    for j in range(4):
        vectors = unpack_vectors(*pairs[j])
        vectors_ref[j, 0], vectors_ref[j, 1] = vectors
        if j > 0:
            factors = unpack_factors(*pairs[j])
            natural = (factors[0].astype(F32) + factors[1].astype(F32)).T
            joint = jnp.concatenate([natural, by_transpose(vectors, factors)], axis=0)
            joint_ref[j - 1, 0], joint_ref[j - 1, 1] = halves(joint)


def plane_kernel(me_ref, *refs, level):
    gots, (joint_ref, vectors_ref, head_ref, send_ref, done_ref) = refs[:4], refs[4:]
    cols = head_ref.shape[0]
    parts = [ref[:cols] for ref in gots]
    heads = [by_place(me_ref[0], parts, j) for j in range(4)]
    for low, high, j in ((0, 1, 1), (2, 3, 3), (0, 2, 2)):
        both = jnp.concatenate([heads[low], heads[high]], axis=1)
        coeffs = plain(halves(both), (joint_ref[j - 1, 0], joint_ref[j - 1, 1]))
        heads[low] = heads[low] - coeffs
        heads[high] = heads[high] - by_transpose(halves(coeffs), (vectors_ref[j, 0], vectors_ref[j, 1]))
    for j in range(4):
        done_ref[j] = heads[j]
    head_ref[...] = heads[0]
    upper = (me_ref[0] >> level) % 2 == 1
    ahead = plain(halves(heads[0]), (vectors_ref[0, 0], vectors_ref[0, 1]))
    fill(send_ref, jnp.where(upper, ahead, heads[0]))


def ready_kernel(me_ref, held_ref, part_ref, part_there_ref, ready_ref, *outs, level):
    me = me_ref[0]
    upper = (me >> level) % 2 == 1
    held = held_ref[0], held_ref[1]
    others = by_core(me % 2, part_ref[...], part_there_ref[...])
    need = held[0].shape[1] // 4 + EXTRA
    node = [jnp.where(upper, a[:need], b[:need]) for a, b in zip(held, others)]
    ready_ref[0], ready_ref[1] = unpack_factors(*node)
    ready_ref[2], ready_ref[3] = unpack_vectors(*held)
    if outs:
        following = [jnp.where(upper, b, a) for a, b in zip(held, others)]
        ready_ref[4], ready_ref[5] = unpack_vectors(*following)
        outs[0][0], outs[0][1] = following


def line_node(me_ref, head_ref, result_ref, mine_ref, there_ref, ready_ref, level):
    me = me_ref[0]
    cols = head_ref.shape[0]
    upper = (me >> level) % 2 == 1
    head, there = head_ref[...], there_ref[:cols]
    coeffs = by_transpose(halves(mine_ref[:cols] + there), (ready_ref[0], ready_ref[1]))
    low = jnp.where(upper, there, head) - coeffs
    plane = me >> 3
    below = (1 << (level - 2)) - 1
    second = (plane & below) == (1 << (level - 3))
    high = head - by_transpose(halves(coeffs), (ready_ref[2], ready_ref[3]))
    return low, jnp.where(second, high, result_ref[...])


def line_kernel(me_ref, *refs, level):
    ready_ref, (head_out, result_out, send_ref) = refs[4], refs[5:]
    low, result = line_node(me_ref, *refs[:5], level)
    ahead = (me_ref[0] >> (level + 1)) % 2 == 1
    head_out[...] = low
    result_out[...] = result
    fill(send_ref, jnp.where(ahead, plain(halves(low), (ready_ref[4], ready_ref[5])), low))


def last_kernel(me_ref, *refs, level):
    done_ref, sends, all_ref = refs[5], refs[6:10], refs[10]
    me = me_ref[0]
    low, result = line_node(me_ref, *refs[:5], level)
    cols = low.shape[0]
    all_ref[0] = jnp.where((me >> 3) == 0, low, result)
    for j in range(1, 4):
        all_ref[j] = done_ref[j]
    for r in range(4):
        sends[r][:cols] = all_ref[place(me) ^ r]
        sends[r][cols:] = low[: sends[r].shape[0] - cols]


def pass_kernel(me_ref, *refs):
    backs, dones, out_ref = refs[:2], refs[2:4], refs[4]
    odd = me_ref[0] % 2 == 1
    cols, rows = dones[0].shape[0], out_ref.shape[1]
    for r in range(2):
        out_ref[r, :cols] = jnp.where(odd, backs[r][:cols], dones[r][...])
        out_ref[r, cols:] = backs[r][cols:rows]


def near_kernel(me_ref, *refs):
    backs, dones, (_, updated_hbm, out_ref, sems) = refs[:4], refs[4:8], refs[8:]
    count, width, half = out_ref.shape
    quarter = half // 4
    me = me_ref[0]
    core = me % 2
    odd = core == 1
    copies = []
    for b in range(count):
        rows = slice(b * quarter, (b + 1) * quarter)
        pieces = [jnp.where(odd, dones[r][rows], backs[r][rows]) for r in range(4)]
        out_ref[b] = jnp.concatenate([by_place(me, pieces, j) for j in range(4)], axis=0).T
        columns = pl.ds(pl.multiple_of(b * width + core * half, half), half)
        copies.append(pltpu.make_async_copy(out_ref.at[b], updated_hbm.at[pl.ds(0, width), columns], sems.at[b]))
        copies[-1].start()
    for copy in copies:
        copy.wait()


def far_kernel(me_ref, *refs, total):
    backs, dones = refs[:4], refs[4:8]
    theres, half_ref, half_there, inverse_ref, _, _, updated_hbm, basis_hbm, gram_hbm = refs[8:10], *refs[10:18]
    panel_ref, sum_ref, out_ref, basis_ref, gram_ref, sems = refs[18:]
    count, width, half = out_ref.shape
    quarter = half // 4
    cols = count * quarter
    me = me_ref[0]
    core = me % 2
    odd = core == 1
    copies = []

    def put(source, target):
        copies.append(pltpu.make_async_copy(source, target, sems.at[len(copies)]))
        copies[-1].start()

    def target(part, r):
        return pl.ds(pl.multiple_of(part * half + (place(me) ^ r) * quarter, quarter), quarter)

    for r in range(4):
        panel_ref[target(core, r)] = backs[r][cols : cols + quarter]
        panel_ref[target(1 - core, r)] = theres[r // 2][r % 2, cols:]
    sum_ref[pl.ds(pl.multiple_of(core * half, half), half)] = half_ref[...]
    sum_ref[pl.ds(pl.multiple_of((1 - core) * half, half), half)] = half_there[...]
    panel = halves(panel_ref[...])
    gram_ref[...] = (sum_ref[...] - by_transpose(panel, panel)) / total
    put(gram_ref, gram_hbm)
    for b in range(count):
        rows = slice(b * quarter, (b + 1) * quarter)
        pieces = [theres[r // 2][r % 2, rows] for r in range(4)]
        far = jnp.concatenate([by_place(me, pieces, j) for j in range(4)], axis=0).T
        out_ref[b] = far
        columns = pl.ds(pl.multiple_of(b * width + (1 - core) * half, half), half)
        put(out_ref.at[b], updated_hbm.at[pl.ds(0, width), columns])
        if b == 0:
            pieces = [jnp.where(odd, dones[r][rows], backs[r][rows]) for r in range(4)]
            near = jnp.concatenate([by_place(me, pieces, j) for j in range(4)], axis=0).T
            head = jnp.concatenate(by_core(core, near, far), axis=1)
            basis = plain(halves(head), halves(inverse_ref[...]))
            basis_ref[...] = jnp.where(me == 0, 0.0, basis)
            put(basis_ref, basis_hbm.at[pl.ds(0, width)])
    for copy in copies:
        copy.wait()


def body(trailing, leaf_vectors, leaf_factors, tree_vectors, tree_factors, inverse_factor):
    rows, columns = trailing.shape
    width = leaf_vectors.shape[1]
    half = width // 2
    quarter = half // 4
    count = columns // width
    devices = lax.axis_size("rows")
    levels = devices.bit_length() - 1
    me = lax.axis_index("rows").astype(jnp.int32)
    me_array = me.reshape(1)
    part_shape = (half + EXTRA, width)
    latest = []

    def exchange(value, shift):
        return lax.ppermute(value, "rows", [(i, i ^ shift) for i in range(devices)])

    def among(value, shift, member):
        return lax.ppermute(value, "rows", [(i, i ^ shift if member(i) else i) for i in range(devices)])

    def around(values):
        there = [exchange(values[r], 2 * r) for r in (3, 1, 2)]
        return [values[0], there[1], there[2], there[0]]

    def shape(*dims):
        return jax.ShapeDtypeStruct(dims, F32)

    def vmem(*dims):
        return pltpu.VMEM(dims, F32)

    def sems(number):
        return pltpu.SemaphoreType.DMA((number,))

    def call(kernel, operands, outs, scratch=(), away_in=(), away_out=(), aliases=(), before=(), work=1, chained=True):
        number = len(operands)
        operands = [pltpu.with_memory_space_constraint(x, pltpu.HBM) if i in away_in else x for i, x in enumerate(operands)]
        outs = [(pltpu.HBM if i in away_out else pltpu.VMEM)(x.shape, x.dtype) for i, x in enumerate(outs)]
        unused = [*latest, *before] if chained else []

        def kernel_on(*refs):
            kernel(*refs[: number + 1], *refs[number + 1 + len(unused) :])

        values = pl.pallas_call(
            kernel_on,
            out_shape=tuple(outs),
            in_specs=[SCALAR]
            + [AWAY if i in away_in else WHOLE for i in range(number)]
            + [pl.BlockSpec(memory_space=pl.ANY)] * len(unused),
            out_specs=tuple(AWAY if i in away_out else WHOLE for i in range(len(outs))),
            scratch_shapes=list(scratch),
            input_output_aliases=dict(aliases),
            compiler_params=PARAMS,
            cost_estimate=pl.CostEstimate(flops=work, bytes_accessed=1, transcendentals=0),
        )(me_array, *operands, *unused)
        if chained and 0 not in away_out:
            latest[:] = values[:1]
        return values

    raw = [exchange(tree_vectors, 1), exchange(tree_factors, 1)]
    blocks = count // 2
    more = count - blocks
    both = jax.ShapeDtypeStruct((2, width, rows), BF16), jax.ShapeDtypeStruct((2, rows, width), BF16)
    rows_a = blocks * half + half
    own_a, away_one, away_two, rest_a, later, inverse_factor, across, combined = call(
        leaf_first_kernel, (trailing, leaf_vectors, leaf_factors, inverse_factor),
        [shape(rows_a, width), shape(rows_a // 2, width), shape(rows_a // 2, width)]
        + [shape(blocks, width, width), shape(more, rows, width), shape(width, width), *both],
        [
            vmem(blocks, rows, width), vmem(rows, width), vmem(width, width), vmem(width, width), vmem(rows_a, width),
            sems(count * (rows // width) + 3),
        ],
        range(4),
    )
    there_a = [exchange(away_one, 1), exchange(away_two, 1)]

    chip_low, chip_high, chip_part = call(
        pack_kernel, (tree_vectors, tree_factors, *raw),
        (shape(2, *part_shape), shape(2, *part_shape), shape(*part_shape)),
        [vmem(4, width, width), sems(4)], (),
    )
    plane_parts = [exchange(chip_part, 2 * r) for r in (3, 1, 2)]
    plane_parts = [plane_parts[1], plane_parts[2], plane_parts[0]]

    own_b, rest_b, *aways = call(
        leaf_second_kernel, (later, across, combined),
        [shape(more * half, width), shape(more, width, width)] + [shape(half, width)] * more,
        [vmem(width, width)], before=there_a,
    )
    theres = [exchange(away, 1) for away in aways]
    cols = count * quarter
    outs = call(
        core_kernel, (own_a, own_b, *there_a, *theres, chip_high),
        [shape(cols, width)] * 3 + [shape(cols + 8, width)] + [shape(cols, width)] * 4 + [shape(half, width)],
        [vmem(count * half, width), vmem(count * half, width)],
    )
    sends, dones, gram_half = outs[:4], outs[4:8], outs[8]
    for level in (levels - 1, 1, 2, *range(3, levels - 1)):
        (gram_half,) = call(
            add_kernel, (gram_half, exchange(gram_half, 1 << level)), (shape(half, width),), chained=False
        )
    stack, held_part = call(
        gather_kernel, (chip_part, *plane_parts), (shape(3, *part_shape), shape(*part_shape)), work=1,
    )
    gots = around(sends)
    stack_there = exchange(stack, 1)
    parts = [exchange(held_part, 8)]
    for level in range(4, levels):
        short = half // 2 + EXTRA if level == levels - 1 else half + EXTRA
        (held_part,) = call(
            functools.partial(hold_kernel, level=level - 1), (held_part, parts[-1]), (shape(short, width),),
            chained=False,
        )
        parts.append(exchange(held_part, 1 << level))

    def split(*dims):
        return jax.ShapeDtypeStruct(dims, BF16)

    joint, vectors, held = call(
        prepare_kernel, (chip_low, stack, stack_there),
        (split(3, 2, 2 * width, width), split(4, 2, width, width), shape(2, *part_shape)),
    )
    head, send, plane_done = call(
        functools.partial(plane_kernel, level=3), (*gots, joint, vectors),
        (shape(cols, width), shape(cols + 24, width), shape(4, cols, width)),
    )
    result = head
    for level in range(3, levels):
        part = parts[level - 3]
        last = level == levels - 1
        ready, *helds = call(
            functools.partial(ready_kernel, level=level), (held, part, exchange(part, 1)),
            [split(4 if last else 6, width, width)] + ([] if last else [shape(2, *part_shape)]),
        )
        operands = (head, result, send, exchange(send, 1 << level), ready)
        if last:
            _, updated, basis = call(
                store_kernel, (rest_a, rest_b, inverse_factor), (shape(8, width), shape(rows, columns), shape(rows, width)),
                [vmem(width, width), sems(count + 1)], (), (1, 2),
            )
            sends = call(
                functools.partial(last_kernel, level=level), (*operands, plane_done),
                [shape(cols + quarter, width)] * 3 + [shape(cols + quarter + 8, width)], [vmem(4, cols, width)],
            )
        else:
            (held,) = helds
            head, result, send = call(
                functools.partial(line_kernel, level=level), operands,
                [shape(cols, width), shape(cols, width), shape(cols, width)],
            )

    backs = around(sends)
    gram_there = exchange(gram_half, 1)
    theres = []
    for r in (0, 2):
        (passed,) = call(
            pass_kernel, (*backs[r : r + 2], *dones[r : r + 2]), (shape(2, cols + quarter, width),),
            before=(gram_half,) if r == 2 else (),
        )
        theres.append(exchange(passed, 1))
    (updated,) = call(
        near_kernel, (*backs, *dones, updated), (shape(rows, columns),),
        [vmem(count, width, half), sems(count)], (8,), (0,), {9: 0},
    )
    return call(
        functools.partial(far_kernel, total=float(rows * devices)),
        (*backs, *dones, *theres, gram_half, gram_there, inverse_factor, updated, basis),
        (shape(rows, columns), shape(rows, width), shape(width, width)),
        [vmem(width, width), vmem(width, width), vmem(count, width, half), vmem(width, width), vmem(width, width), sems(count + 2)],
        (13, 14), (0, 1, 2), {14: 0, 15: 1},
    )


def solution(mesh):
    in_specs = (
        P("rows", None),
        P("rows", None),
        P("rows", None),
        P("rows", None),
        P("rows", None),
        P(),
    )
    out_specs = (P("rows", None), P("rows", None), P())
    return jax.shard_map(body, mesh=mesh, in_specs=in_specs, out_specs=out_specs, check_vma=False)
```

profile of v0, /device:TPU:0, one launch (start us, length us, event | category | flops | bytes accessed | tf_op | source)
XLA Modules:
  0.0 59.4 jit_solution(5635648116133997967)
XLA Ops:
  1.2 4.2 %shard_map.85 = (f32[384,256]{1,0:T(8,128)S(1)}, f32[192,256]{1,0:T(8,128)S(1)}, f32[192,256]{1,0:T(8,128)S(1)}, f32[2,256,256]{2,1,0:T(8,128)S(1)}, f32[2,512,2...) custom-call(s32[1]{0:T(128)} %bitcast.refs_0_, ...), custom_call_target="tpu_custom_call" | custom-call | flops 1 | bytes 1 | tf_op jit(solution)/shard_map/pallas_call | solution.py:473
  6.4 3.9 %collective-permute-start.11 = (f32[136,256]{1,0:T(8,128)S(1)}, f32[136,256]{1,0:T(8,128)S(1)}, u32[]{:S(2)}, u32[]{:S(2)}) collective-permute-start(f32[136,256]{1,0:T(8,128)S(1)} %get-tuple-element.62.refs_1_), channel_id=1, source_target_pairs={{0,6},{1,7},{2,4},{3,5},{4,2},{5,3},{6,0},{7,1},{8,14},{9,15},{10,... | collective-permute-start | bytes 417800 | tf_op jit(solution)/shard_map/ppermute | solution.py:446
  10.9 1.6 %shard_map.87 = (f32[256,256]{1,0:T(8,128)S(1)}, f32[2,256,256]{2,1,0:T(8,128)S(1)}, f32[128,256]{1,0:T(8,128)S(1)}, f32[128,256]{1,0:T(8,128)S(1)}) custom-call(s32[1]{0:T(128)} %bitcast.refs_0_, f32[2,512,256]{2,1,0:T(8,128)S(1)} %get-tuple-element.48.refs_1_, bf16[2,256,512]{2,1,0:T(8,128)(2,1)S(1)} %get-tuple-element.49.refs_2_, ...), custom_call_target="tpu_custom_call" | custom-call | flops 1 | bytes 1 | tf_op jit(solution)/shard_map/pallas_call | solution.py:473
  14.1 1.3 %shard_map.88 = (f32[128,256]{1,0:T(8,128)S(1)}, f32[128,256]{1,0:T(8,128)S(1)}, f32[128,256]{1,0:T(8,128)S(1)}, f32[136,256]{1,0:T(8,128)S(1)}, f32[128,256]{1,...) custom-call(s32[1]{0:T(128)} %bitcast.refs_0_, ...), custom_call_target="tpu_custom_call" | custom-call | flops 1 | bytes 1 | tf_op jit(solution)/shard_map/pallas_call | solution.py:473
  15.5 1.7 %collective-permute-done.10.refs_3_ = f32[136,256]{1,0:T(8,128)S(1)} collective-permute-done((f32[136,256]{1,0:T(8,128)S(1)}, f32[136,256]{1,0:T(8,128)S(1)}, u32[]{:S(2)}, u32[]{:S(2)}) %collective-permute-start.10) | collective-permute-done | bytes 139296 | tf_op jit(solution)/shard_map/ppermute | solution.py:446
  17.6 1.6 %collective-permute-start.8 = (f32[136,256]{1,0:T(8,128)S(1)}, f32[136,256]{1,0:T(8,128)S(1)}, u32[]{:S(2)}, u32[]{:S(2)}) collective-permute-start(f32[136,256]{1,0:T(8,128)S(1)} %get-tuple-element.61), channel_id=1, source_target_pairs={{0,6},{1,7},{2,4},{3,5},{4,2},{5,3},{6,0},{7,1},{8,14},{9,15},{10,... | collective-permute-start | bytes 417800 | tf_op jit(solution)/shard_map/ppermute | solution.py:446
  19.2 1.4 %collective-permute-start.6 = (f32[128,256]{1,0:T(8,128)S(1)}, f32[128,256]{1,0:T(8,128)S(1)}, u32[]{:S(2)}, u32[]{:S(2)}) collective-permute-start(f32[128,256]{1,0:T(8,128)S(1)} %get-tuple-element.59), channel_id=1, source_target_pairs={{0,2},{1,3},{2,0},{3,1},{4,6},{5,7},{6,4},{7,5},{8,10},{9,11},{10,... | collective-permute-start | bytes 393224 | tf_op jit(solution)/shard_map/ppermute | solution.py:446
  21.2 1.6 %collective-permute-start.14 = (f32[136,256]{1,0:T(8,128)S(1)}, f32[136,256]{1,0:T(8,128)S(1)}, u32[]{:S(2)}, u32[]{:S(2)}) collective-permute-start(f32[136,256]{1,0:T(8,128)S(1)} %get-tuple-element.69.refs_1_), channel_id=1, source_target_pairs={{0,8},{1,9},{2,10},{3,11},{4,12},{5,13},{6,14},{7,15},{8,0},{9,1},... | collective-permute-start | bytes 417800 | tf_op jit(solution)/shard_map/ppermute | solution.py:446
  22.8 2.6 %collective-permute-start.23 = (f32[128,256]{1,0:T(8,128)S(1)}, f32[128,256]{1,0:T(8,128)S(1)}, u32[]{:S(2)}, u32[]{:S(2)}) collective-permute-start(f32[128,256]{1,0:T(8,128)S(1)} %get-tuple-element.88.refs_1_), channel_id=1, source_target_pairs={{0,16},{1,17},{2,18},{3,19},{4,20},{5,21},{6,22},{7,23},{8,24},{9,... | collective-permute-start | bytes 393224 | tf_op jit(solution)/shard_map/ppermute | solution.py:446
  26.2 1.2 %collective-permute-done.6.refs_2_ = f32[128,256]{1,0:T(8,128)S(1)} collective-permute-done((f32[128,256]{1,0:T(8,128)S(1)}, f32[128,256]{1,0:T(8,128)S(1)}, u32[]{:S(2)}, u32[]{:S(2)}) %collective-permute-start.6) | collective-permute-done | bytes 131104 | tf_op jit(solution)/shard_map/ppermute | solution.py:446
  27.4 1.2 %shard_map.91 = (f32[128,256]{1,0:T(8,128)S(1)}, f32[152,256]{1,0:T(8,128)S(1)}, f32[4,128,256]{2,1,0:T(8,128)S(1)}) custom-call(s32[1]{0:T(128)} %bitcast.refs_0_, f32[128,256]{1,0:T(8,128)S(1)} %get-tuple-element.58.refs_5_.refs_1_, f32[128,256]{1,0:T(8,128)S(1)} %collective-permute-done.6.refs_2_, f32[128,256]{1,0:T(8,128)S(1)} %collective-permute-done.7.refs_3_, ...), custom_call_target="tpu_custom_call" | custom-call | flops 1 | bytes 1 | tf_op jit(solution)/shard_map/pallas_call | solution.py:473
  28.6 1.6 %collective-permute-start.13 = (f32[152,256]{1,0:T(8,128)S(1)}, f32[152,256]{1,0:T(8,128)S(1)}, u32[]{:S(2)}, u32[]{:S(2)}) collective-permute-start(f32[152,256]{1,0:T(8,128)S(1)} %get-tuple-element.67.refs_3_), channel_id=1, source_target_pairs={{0,8},{1,9},{2,10},{3,11},{4,12},{5,13},{6,14},{7,15},{8,0},{9,1},... | collective-permute-start | bytes 466952 | tf_op jit(solution)/shard_map/ppermute | solution.py:446
  30.3 1.2 %collective-permute-done.23.refs_2_ = f32[128,256]{1,0:T(8,128)S(1)} collective-permute-done((f32[128,256]{1,0:T(8,128)S(1)}, f32[128,256]{1,0:T(8,128)S(1)}, u32[]{:S(2)}, u32[]{:S(2)}) %collective-permute-start.23) | collective-permute-done | bytes 131104 | tf_op jit(solution)/shard_map/ppermute | solution.py:446
  31.4 1.6 %collective-permute-start.24 = (f32[128,256]{1,0:T(8,128)S(1)}, f32[128,256]{1,0:T(8,128)S(1)}, u32[]{:S(2)}, u32[]{:S(2)}) collective-permute-start(f32[128,256]{1,0:T(8,128)S(1)} %shard_map.99.refs_1_), channel_id=1, source_target_pairs={{0,2},{1,3},{2,0},{3,1},{4,6},{5,7},{6,4},{7,5},{8,10},{9,11},{10,... | collective-permute-start | bytes 393224 | tf_op jit(solution)/shard_map/ppermute | solution.py:446
  33.0 1.5 %collective-permute-start.17 = (f32[72,256]{1,0:T(8,128)S(1)}, f32[72,256]{1,0:T(8,128)S(1)}, u32[]{:S(2)}, u32[]{:S(2)}) collective-permute-start(f32[72,256]{1,0:T(8,128)S(1)} %shard_map.94), channel_id=1, source_target_pairs={{0,16},{1,17},{2,18},{3,19},{4,20},{5,21},{6,22},{7,23},{8,24},{9,... | collective-permute-start | bytes 221192 | tf_op jit(solution)/shard_map/ppermute | solution.py:446
  35.3 3.4 %collective-permute-start.16 = (f32[128,256]{1,0:T(8,128)S(1)}, f32[128,256]{1,0:T(8,128)S(1)}, u32[]{:S(2)}, u32[]{:S(2)}) collective-permute-start(f32[128,256]{1,0:T(8,128)S(1)} %get-tuple-element.73.refs_3_), channel_id=1, source_target_pairs={{0,16},{1,17},{2,18},{3,19},{4,20},{5,21},{6,22},{7,23},{8,24},{9,... | collective-permute-start | bytes 393224 | tf_op jit(solution)/shard_map/ppermute | solution.py:446
  38.7 1.5 %collective-permute-start.25 = (f32[128,256]{1,0:T(8,128)S(1)}, f32[128,256]{1,0:T(8,128)S(1)}, u32[]{:S(2)}, u32[]{:S(2)}) collective-permute-start(f32[128,256]{1,0:T(8,128)S(1)} %shard_map.100.refs_1_), channel_id=1, source_target_pairs={{0,4},{1,5},{2,6},{3,7},{4,0},{5,1},{6,2},{7,3},{8,12},{9,13},{10,... | collective-permute-start | bytes 393224 | tf_op jit(solution)/shard_map/ppermute | solution.py:446
  40.6 1.3 %collective-permute-done.18.refs_3_ = f32[72,256]{1,0:T(8,128)S(1)} collective-permute-done((f32[72,256]{1,0:T(8,128)S(1)}, f32[72,256]{1,0:T(8,128)S(1)}, u32[]{:S(2)}, u32[]{:S(2)}) %collective-permute-start.18) | collective-permute-done | bytes 73760 | tf_op jit(solution)/shard_map/ppermute | solution.py:446
  42.0 1.1 %shard_map.96 = (f32[8,256]{1,0:T(8,128)S(1)}, f32[512,1024]{1,0:T(8,128)}, f32[512,256]{1,0:T(8,128)}) custom-call(s32[1]{0:T(128)} %bitcast.refs_0_, f32[2,256,256]{2,1,0:T(8,128)S(1)} %get-tuple-element.76.refs_1_, f32[2,256,256]{2,1,0:T(8,128)S(1)} %get-tuple-element.77.refs_2_, f32[256,256]{1,0:T(8,128)S(1)} %get-tuple-element.78.refs_3_.refs_13_, ...), custom_call_target="tpu_custom_call" | custom-call | flops 1 | bytes 1 | tf_op jit(solution)/shard_map/pallas_call | solution.py:473
  43.1 1.5 %collective-permute-done.16.refs_4_ = f32[128,256]{1,0:T(8,128)S(1)} collective-permute-done((f32[128,256]{1,0:T(8,128)S(1)}, f32[128,256]{1,0:T(8,128)S(1)}, u32[]{:S(2)}, u32[]{:S(2)}) %collective-permute-start.16) | collective-permute-done | bytes 131104 | tf_op jit(solution)/shard_map/ppermute | solution.py:446
  45.3 1.6 %collective-permute-start.21 = (f32[168,256]{1,0:T(8,128)S(1)}, f32[168,256]{1,0:T(8,128)S(1)}, u32[]{:S(2)}, u32[]{:S(2)}) collective-permute-start(f32[168,256]{1,0:T(8,128)S(1)} %get-tuple-element.83), channel_id=1, source_target_pairs={{0,6},{1,7},{2,4},{3,5},{4,2},{5,3},{6,0},{7,1},{8,14},{9,15},{10,... | collective-permute-start | bytes 516104 | tf_op jit(solution)/shard_map/ppermute | solution.py:446
  49.0 5.0 %collective-permute-done.26.refs_2_ = f32[128,256]{1,0:T(8,128)S(1)} collective-permute-done((f32[128,256]{1,0:T(8,128)S(1)}, f32[128,256]{1,0:T(8,128)S(1)}, u32[]{:S(2)}, u32[]{:S(2)}) %collective-permute-start.26) | collective-permute-done | bytes 131104 | tf_op jit(solution)/shard_map/ppermute | solution.py:446
  53.9 1.4 %collective-permute-done.19.refs_2_ = f32[160,256]{1,0:T(8,128)S(1)} collective-permute-done((f32[160,256]{1,0:T(8,128)S(1)}, f32[160,256]{1,0:T(8,128)S(1)}, u32[]{:S(2)}, u32[]{:S(2)}) %collective-permute-start.19) | collective-permute-done | bytes 163872 | tf_op jit(solution)/shard_map/ppermute | solution.py:446
  57.9 1.5 %shard_map.105 = (f32[512,1024]{1,0:T(8,128)}, f32[512,256]{1,0:T(8,128)}, f32[256,256]{1,0:T(8,128)}) custom-call(s32[1]{0:T(128)} %bitcast.refs_0_, f32[160,256]{1,0:T(8,128)S(1)} %get-tuple-element.80.refs_1_.refs_5_, f32[160,256]{1,0:T(8,128)S(1)} %collective-permute-done.19.refs_2_, ...), custom_call_target="tpu_custom_call", output_to_operand_aliasing={{0}: (14, {}), {1}: (15, {})} | custom-call | flops 1 | bytes 1 | tf_op jit(solution)/shard_map/pallas_call | solution.py:473
  (59 shorter events, 12.4 us)
Async XLA Ops:
  0.7 5.4 %collective-permute-start = (f32[256,256]{1,0:T(8,128)}, f32[256,256]{1,0:T(8,128)S(1)}, u32[]{:S(2)}, u32[]{:S(2)}) collective-permute-start(f32[256,256]{1,0:T(8,128)} %refs_1_.3), channel_id=1, source_target_pairs={{0,1},{1,0},{2,3},{3,2},{4,5},{5,4},{6,7},{7,6},{8,9},{9,8},{10,11... | collective-permute-start | bytes 786440 | tf_op jit(solution)/shard_map/ppermute | solution.py:446
  1.2 4.8 %collective-permute-start.1 = (f32[256,256]{1,0:T(8,128)}, f32[256,256]{1,0:T(8,128)S(1)}, u32[]{:S(2)}, u32[]{:S(2)}) collective-permute-start(f32[256,256]{1,0:T(8,128)} %refs_2_.3), channel_id=1, source_target_pairs={{0,1},{1,0},{2,3},{3,2},{4,5},{5,4},{6,7},{7,6},{8,9},{9,8},{10,11... | collective-permute-start | bytes 786440 | tf_op jit(solution)/shard_map/ppermute | solution.py:446
  5.4 5.5 %collective-permute-start.2 = (f32[192,256]{1,0:T(8,128)S(1)}, f32[192,256]{1,0:T(8,128)S(1)}, u32[]{:S(2)}, u32[]{:S(2)}) collective-permute-start(f32[192,256]{1,0:T(8,128)S(1)} %get-tuple-element.52), channel_id=1, source_target_pairs={{0,1},{1,0},{2,3},{3,2},{4,5},{5,4},{6,7},{7,6},{8,9},{9,8},{10,11... | collective-permute-start | bytes 589832 | tf_op jit(solution)/shard_map/ppermute | solution.py:446
  5.9 5.0 %collective-permute-start.3 = (f32[192,256]{1,0:T(8,128)S(1)}, f32[192,256]{1,0:T(8,128)S(1)}, u32[]{:S(2)}, u32[]{:S(2)}) collective-permute-start(f32[192,256]{1,0:T(8,128)S(1)} %get-tuple-element.53), channel_id=1, source_target_pairs={{0,1},{1,0},{2,3},{3,2},{4,5},{5,4},{6,7},{7,6},{8,9},{9,8},{10,11... | collective-permute-start | bytes 589832 | tf_op jit(solution)/shard_map/ppermute | solution.py:446
  6.4 9.1 %collective-permute-start.11 = (f32[136,256]{1,0:T(8,128)S(1)}, f32[136,256]{1,0:T(8,128)S(1)}, u32[]{:S(2)}, u32[]{:S(2)}) collective-permute-start(f32[136,256]{1,0:T(8,128)S(1)} %get-tuple-element.62.refs_1_), channel_id=1, source_target_pairs={{0,6},{1,7},{2,4},{3,5},{4,2},{5,3},{6,0},{7,1},{8,14},{9,15},{10,... | collective-permute-start | bytes 417800 | tf_op jit(solution)/shard_map/ppermute | solution.py:446
  10.3 6.9 %collective-permute-start.10 = (f32[136,256]{1,0:T(8,128)S(1)}, f32[136,256]{1,0:T(8,128)S(1)}, u32[]{:S(2)}, u32[]{:S(2)}) collective-permute-start(f32[136,256]{1,0:T(8,128)S(1)} %get-tuple-element.62.refs_1_), channel_id=1, source_target_pairs={{0,4},{1,5},{2,6},{3,7},{4,0},{5,1},{6,2},{7,3},{8,12},{9,13},{10,... | collective-permute-start | bytes 417800 | tf_op jit(solution)/shard_map/ppermute | solution.py:446
  10.8 6.7 %collective-permute-start.9 = (f32[136,256]{1,0:T(8,128)S(1)}, f32[136,256]{1,0:T(8,128)S(1)}, u32[]{:S(2)}, u32[]{:S(2)}) collective-permute-start(f32[136,256]{1,0:T(8,128)S(1)} %get-tuple-element.62.refs_1_), channel_id=1, source_target_pairs={{0,2},{1,3},{2,0},{3,1},{4,6},{5,7},{6,4},{7,5},{8,10},{9,11},{10,... | collective-permute-start | bytes 417800 | tf_op jit(solution)/shard_map/ppermute | solution.py:446
  17.6 5.2 %collective-permute-start.12 = (f32[3,136,256]{2,1,0:T(8,128)S(1)}, f32[3,136,256]{2,1,0:T(8,128)S(1)}, u32[]{:S(2)}, u32[]{:S(2)}) collective-permute-start(f32[3,136,256]{2,1,0:T(8,128)S(1)} %get-tuple-element.63.refs_2_.refs_4_), channel_id=1, source_target_pairs={{0,1},{1,0},{2,3},{3,2},{4,5},{5,4},{6,7},{7,6},{8,9},{9,8},{10,11... | collective-permute-start | bytes 1253384 | tf_op jit(solution)/shard_map/ppermute | solution.py:446
  17.6 9.8 %collective-permute-start.8 = (f32[136,256]{1,0:T(8,128)S(1)}, f32[136,256]{1,0:T(8,128)S(1)}, u32[]{:S(2)}, u32[]{:S(2)}) collective-permute-start(f32[136,256]{1,0:T(8,128)S(1)} %get-tuple-element.61), channel_id=1, source_target_pairs={{0,6},{1,7},{2,4},{3,5},{4,2},{5,3},{6,0},{7,1},{8,14},{9,15},{10,... | collective-permute-start | bytes 417800 | tf_op jit(solution)/shard_map/ppermute | solution.py:446
  19.2 8.2 %collective-permute-start.6 = (f32[128,256]{1,0:T(8,128)S(1)}, f32[128,256]{1,0:T(8,128)S(1)}, u32[]{:S(2)}, u32[]{:S(2)}) collective-permute-start(f32[128,256]{1,0:T(8,128)S(1)} %get-tuple-element.59), channel_id=1, source_target_pairs={{0,2},{1,3},{2,0},{3,1},{4,6},{5,7},{6,4},{7,5},{8,10},{9,11},{10,... | collective-permute-start | bytes 393224 | tf_op jit(solution)/shard_map/ppermute | solution.py:446
  20.6 6.9 %collective-permute-start.7 = (f32[128,256]{1,0:T(8,128)S(1)}, f32[128,256]{1,0:T(8,128)S(1)}, u32[]{:S(2)}, u32[]{:S(2)}) collective-permute-start(f32[128,256]{1,0:T(8,128)S(1)} %get-tuple-element.60), channel_id=1, source_target_pairs={{0,4},{1,5},{2,6},{3,7},{4,0},{5,1},{6,2},{7,3},{8,12},{9,13},{10,... | collective-permute-start | bytes 393224 | tf_op jit(solution)/shard_map/ppermute | solution.py:446
  21.2 9.1 %collective-permute-start.14 = (f32[136,256]{1,0:T(8,128)S(1)}, f32[136,256]{1,0:T(8,128)S(1)}, u32[]{:S(2)}, u32[]{:S(2)}) collective-permute-start(f32[136,256]{1,0:T(8,128)S(1)} %get-tuple-element.69.refs_1_), channel_id=1, source_target_pairs={{0,8},{1,9},{2,10},{3,11},{4,12},{5,13},{6,14},{7,15},{8,0},{9,1},... | collective-permute-start | bytes 417800 | tf_op jit(solution)/shard_map/ppermute | solution.py:446
  22.8 8.7 %collective-permute-start.23 = (f32[128,256]{1,0:T(8,128)S(1)}, f32[128,256]{1,0:T(8,128)S(1)}, u32[]{:S(2)}, u32[]{:S(2)}) collective-permute-start(f32[128,256]{1,0:T(8,128)S(1)} %get-tuple-element.88.refs_1_), channel_id=1, source_target_pairs={{0,16},{1,17},{2,18},{3,19},{4,20},{5,21},{6,22},{7,23},{8,24},{9,... | collective-permute-start | bytes 393224 | tf_op jit(solution)/shard_map/ppermute | solution.py:446
  28.6 6.1 %collective-permute-start.13 = (f32[152,256]{1,0:T(8,128)S(1)}, f32[152,256]{1,0:T(8,128)S(1)}, u32[]{:S(2)}, u32[]{:S(2)}) collective-permute-start(f32[152,256]{1,0:T(8,128)S(1)} %get-tuple-element.67.refs_3_), channel_id=1, source_target_pairs={{0,8},{1,9},{2,10},{3,11},{4,12},{5,13},{6,14},{7,15},{8,0},{9,1},... | collective-permute-start | bytes 466952 | tf_op jit(solution)/shard_map/ppermute | solution.py:446
  30.3 4.3 %collective-permute-start.15 = (f32[136,256]{1,0:T(8,128)S(1)}, f32[136,256]{1,0:T(8,128)S(1)}, u32[]{:S(2)}, u32[]{:S(2)}) collective-permute-start(f32[136,256]{1,0:T(8,128)S(1)} %collective-permute-done.14.refs_2_), channel_id=1, source_target_pairs={{0,1},{1,0},{2,3},{3,2},{4,5},{5,4},{6,7},{7,6},{8,9},{9,8},{10,11... | collective-permute-start | bytes 417800 | tf_op jit(solution)/shard_map/ppermute | solution.py:446
  31.4 7.2 %collective-permute-start.24 = (f32[128,256]{1,0:T(8,128)S(1)}, f32[128,256]{1,0:T(8,128)S(1)}, u32[]{:S(2)}, u32[]{:S(2)}) collective-permute-start(f32[128,256]{1,0:T(8,128)S(1)} %shard_map.99.refs_1_), channel_id=1, source_target_pairs={{0,2},{1,3},{2,0},{3,1},{4,6},{5,7},{6,4},{7,5},{8,10},{9,11},{10,... | collective-permute-start | bytes 393224 | tf_op jit(solution)/shard_map/ppermute | solution.py:446
  33.0 7.6 %collective-permute-start.17 = (f32[72,256]{1,0:T(8,128)S(1)}, f32[72,256]{1,0:T(8,128)S(1)}, u32[]{:S(2)}, u32[]{:S(2)}) collective-permute-start(f32[72,256]{1,0:T(8,128)S(1)} %shard_map.94), channel_id=1, source_target_pairs={{0,16},{1,17},{2,18},{3,19},{4,20},{5,21},{6,22},{7,23},{8,24},{9,... | collective-permute-start | bytes 221192 | tf_op jit(solution)/shard_map/ppermute | solution.py:446
  35.3 9.3 %collective-permute-start.16 = (f32[128,256]{1,0:T(8,128)S(1)}, f32[128,256]{1,0:T(8,128)S(1)}, u32[]{:S(2)}, u32[]{:S(2)}) collective-permute-start(f32[128,256]{1,0:T(8,128)S(1)} %get-tuple-element.73.refs_3_), channel_id=1, source_target_pairs={{0,16},{1,17},{2,18},{3,19},{4,20},{5,21},{6,22},{7,23},{8,24},{9,... | collective-permute-start | bytes 393224 | tf_op jit(solution)/shard_map/ppermute | solution.py:446
  38.7 10.2 %collective-permute-start.25 = (f32[128,256]{1,0:T(8,128)S(1)}, f32[128,256]{1,0:T(8,128)S(1)}, u32[]{:S(2)}, u32[]{:S(2)}) collective-permute-start(f32[128,256]{1,0:T(8,128)S(1)} %shard_map.100.refs_1_), channel_id=1, source_target_pairs={{0,4},{1,5},{2,6},{3,7},{4,0},{5,1},{6,2},{7,3},{8,12},{9,13},{10,... | collective-permute-start | bytes 393224 | tf_op jit(solution)/shard_map/ppermute | solution.py:446
  45.3 10.7 %collective-permute-start.21 = (f32[168,256]{1,0:T(8,128)S(1)}, f32[168,256]{1,0:T(8,128)S(1)}, u32[]{:S(2)}, u32[]{:S(2)}) collective-permute-start(f32[168,256]{1,0:T(8,128)S(1)} %get-tuple-element.83), channel_id=1, source_target_pairs={{0,6},{1,7},{2,4},{3,5},{4,2},{5,3},{6,0},{7,1},{8,14},{9,15},{10,... | collective-permute-start | bytes 516104 | tf_op jit(solution)/shard_map/ppermute | solution.py:446
  46.9 8.4 %collective-permute-start.19 = (f32[160,256]{1,0:T(8,128)S(1)}, f32[160,256]{1,0:T(8,128)S(1)}, u32[]{:S(2)}, u32[]{:S(2)}) collective-permute-start(f32[160,256]{1,0:T(8,128)S(1)} %get-tuple-element.81), channel_id=1, source_target_pairs={{0,2},{1,3},{2,0},{3,1},{4,6},{5,7},{6,4},{7,5},{8,10},{9,11},{10,... | collective-permute-start | bytes 491528 | tf_op jit(solution)/shard_map/ppermute | solution.py:446
  47.9 8.1 %collective-permute-start.20 = (f32[160,256]{1,0:T(8,128)S(1)}, f32[160,256]{1,0:T(8,128)S(1)}, u32[]{:S(2)}, u32[]{:S(2)}) collective-permute-start(f32[160,256]{1,0:T(8,128)S(1)} %get-tuple-element.82), channel_id=1, source_target_pairs={{0,4},{1,5},{2,6},{3,7},{4,0},{5,1},{6,2},{7,3},{8,12},{9,13},{10,... | collective-permute-start | bytes 491528 | tf_op jit(solution)/shard_map/ppermute | solution.py:446
  48.9 5.0 %collective-permute-start.26 = (f32[128,256]{1,0:T(8,128)S(1)}, f32[128,256]{1,0:T(8,128)S(1)}, u32[]{:S(2)}, u32[]{:S(2)}) collective-permute-start(f32[128,256]{1,0:T(8,128)S(1)} %shard_map.101.refs_1_), channel_id=1, source_target_pairs={{0,8},{1,9},{2,10},{3,11},{4,12},{5,13},{6,14},{7,15},{8,0},{9,1},... | collective-permute-start | bytes 393224 | tf_op jit(solution)/shard_map/ppermute | solution.py:446
  55.3 2.6 %collective-permute-start.22 = (f32[2,160,256]{2,1,0:T(8,128)S(1)}, f32[2,160,256]{2,1,0:T(8,128)S(1)}, u32[]{:S(2)}, u32[]{:S(2)}) collective-permute-start(f32[2,160,256]{2,1,0:T(8,128)S(1)} %shard_map.98.refs_5_), channel_id=1, source_target_pairs={{0,1},{1,0},{2,3},{3,2},{4,5},{5,4},{6,7},{7,6},{8,9},{9,8},{10,11... | collective-permute-start | bytes 983048 | tf_op jit(solution)/shard_map/ppermute | solution.py:446
  (7 other events, 18.6 us)
where the time goes:
time: 59.6 us; the launch traced here: 59.4 us
  starting transfers between devices  27.9 us (47%)
  waiting for transfers between devices  15.9 us (27%)
  Pallas kernels  14.7 us (25%)
  between operations  0.83 us (1%)
    ppermute x29, starting transfers between devices, exchange(): return lax.ppermute(value, 'rows', [(i, i ^ shift) for i in range(devices)])  27.9 us
    ppermute x29, waiting for transfers between devices, exchange(): return lax.ppermute(value, 'rows', [(i, i ^ shift) for i in range(devices)])  15.9 us
    pallas_call x21, Pallas kernels, call(): pl.pallas_call(kernel_on, out_shape=tuple(outs), in_specs=[SCALAR] + [AWA...  14.7 us
  transfers between devices with their start and end apart: 29, of which 13 were waited for; matrix products, arithmetic and copies ran while one was open for 0% of the time, Pallas kernels for 22%

commit v1 on v0

--- a/solution.py
+++ b/solution.py
@@ -214,35 +214,37 @@
         copy.wait()
 
 
-def core_kernel(
-    me_ref, own_a_ref, own_b_ref, one_ref, two_ref, *refs
-):
-    more = len(refs) - 12
-    there_bs, packed_ref = refs[:more], refs[more]
-    sends, dones, (gram_ref, low_ref, high_ref) = refs[more + 1 : more + 5], refs[more + 5 : more + 9], refs[more + 9 :]
+def core_first_kernel(me_ref, own_ref, one_ref, two_ref, packed_ref, low_ref, high_ref, gram_ref):
+    cut = low_ref.shape[0]
+    there = jnp.concatenate([one_ref[...], two_ref[...]], axis=0)
+    gram_ref[...] = own_ref[cut:] + there[cut:]
+    core_node(me_ref, own_ref[:cut], there[:cut], packed_ref, low_ref, high_ref)
+
+
+def core_node(me_ref, mine, there, packed_ref, low_ref, high_ref):
+    odd = me_ref[0] % 2 == 1
+    low, high = jnp.where(odd, there, mine), jnp.where(odd, mine, there)
+    low_ref[...], high_ref[...] = tree_node(low, high, unpack(packed_ref[0], packed_ref[1]))
+
+
+def core_kernel(me_ref, low_a_ref, high_a_ref, own_ref, *refs):
+    theres, packed_ref, refs = refs[:-11], refs[-11], refs[-10:]
+    sends, dones, (low_ref, high_ref) = refs[:4], refs[4:8], refs[8:]
     me = me_ref[0]
-    width = own_a_ref.shape[1]
-    half = width // 2
+    half = own_ref.shape[1] // 2
     quarter = half // 4
-    cut = own_a_ref.shape[0] - half
-    count = cut // half + len(there_bs)
-    odd = me % 2 == 1
-    there_a = jnp.concatenate([one_ref[...], two_ref[...]], axis=0)
-    gram_ref[...] = own_a_ref[cut:] + there_a[cut:]
-    mine = jnp.concatenate([own_a_ref[:cut], own_b_ref[...]], axis=0)
-    there = jnp.concatenate([there_a[:cut]] + [ref[...] for ref in there_bs], axis=0)
-    low = jnp.where(odd, there, mine)
-    high = jnp.where(odd, mine, there)
-    low, high = tree_node(low, high, unpack(packed_ref[0], packed_ref[1]))
-    low_ref[...] = low
-    high_ref[...] = high
+    there = jnp.concatenate([ref[...] for ref in theres], axis=0)
+    core_node(me_ref, own_ref[...], there, packed_ref, low_ref, high_ref)
+    first = low_a_ref.shape[0] // half
+    count = first + own_ref.shape[0] // half
     for r in range(4):
         start = (place(me) ^ r) * quarter
         for b in range(count):
-            source = pl.ds(pl.multiple_of(b * half + start, quarter), quarter)
+            lows, highs, block = (low_a_ref, high_a_ref, b) if b < first else (low_ref, high_ref, b - first)
+            source = pl.ds(pl.multiple_of(block * half + start, quarter), quarter)
             target = slice(b * quarter, (b + 1) * quarter)
-            sends[r][target] = low_ref[source]
-            dones[r][target] = high_ref[source]
+            sends[r][target] = lows[source]
+            dones[r][target] = highs[source]
         if sends[r].shape[0] > count * quarter:
             sends[r][count * quarter :] = jnp.zeros_like(sends[r][count * quarter :])
 
@@ -518,12 +520,16 @@
     )
     theres = [exchange(away, 1) for away in aways]
     cols = count * quarter
+    low_a, high_a, gram_half = call(
+        core_first_kernel, (own_a, *there_a, chip_high),
+        [shape(blocks * half, width)] * 2 + [shape(half, width)],
+    )
     outs = call(
-        core_kernel, (own_a, own_b, *there_a, *theres, chip_high),
-        [shape(cols, width)] * 3 + [shape(cols + 8, width)] + [shape(cols, width)] * 4 + [shape(half, width)],
-        [vmem(count * half, width), vmem(count * half, width)],
-    )
-    sends, dones, gram_half = outs[:4], outs[4:8], outs[8]
+        core_kernel, (low_a, high_a, own_b, *theres, chip_high),
+        [shape(cols, width)] * 3 + [shape(cols + 8, width)] + [shape(cols, width)] * 4,
+        [vmem(more * half, width), vmem(more * half, width)],
+    )
+    sends, dones = outs[:4], outs[4:8]
     for level in (levels - 1, 1, 2, *range(3, levels - 1)):
         (gram_half,) = call(
             add_kernel, (gram_half, exchange(gram_half, 1 << level)), (shape(half, width),), chained=False

time: 59.6 us -> 59.6 us (level)
    pallas_call x21 -> x22, Pallas kernels: 14.7 us -> 15.1 us  [call(): pl.pallas_call(kernel_on, out_shape=tuple(outs), in_specs=[SCALAR] + [AWA...]
  transfers between devices with their start and end apart: 29 -> 29, of which waited for: 13 -> 12; matrix products, arithmetic and copies ran while one was open for 0% -> 0% of each run, Pallas kernels for 22% -> 23%
where the time goes in v1:
time: 59.6 us; the launch traced here: 59.4 us
  starting transfers between devices  27.9 us (47%)
  waiting for transfers between devices  15.5 us (26%)
  Pallas kernels  15.1 us (25%)
  between operations  0.84 us (1%)
    ppermute x29, starting transfers between devices, exchange(): return lax.ppermute(value, 'rows', [(i, i ^ shift) for i in range(devices)])  27.9 us
    ppermute x29, waiting for transfers between devices, exchange(): return lax.ppermute(value, 'rows', [(i, i ^ shift) for i in range(devices)])  15.5 us
    pallas_call x22, Pallas kernels, call(): pl.pallas_call(kernel_on, out_shape=tuple(outs), in_specs=[SCALAR] + [AWA...  15.1 us
  transfers between devices with their start and end apart: 29, of which 12 were waited for; matrix products, arithmetic and copies ran while one was open for 0% of the time, Pallas kernels for 23%

profile of v1, /device:TPU:0, one launch (start us, length us, event | category | flops | bytes accessed | tf_op | source)
XLA Modules:
  0.0 59.4 jit_solution(12814478081401645198)
XLA Ops:
  1.2 4.2 %shard_map.85 = (f32[384,256]{1,0:T(8,128)S(1)}, f32[192,256]{1,0:T(8,128)S(1)}, f32[192,256]{1,0:T(8,128)S(1)}, f32[2,256,256]{2,1,0:T(8,128)S(1)}, f32[2,512,2...) custom-call(s32[1]{0:T(128)} %bitcast.refs_0_, ...), custom_call_target="tpu_custom_call" | custom-call | flops 1 | bytes 1 | tf_op jit(solution)/shard_map/pallas_call | solution.py:475
  6.4 3.9 %collective-permute-start.11 = (f32[136,256]{1,0:T(8,128)S(1)}, f32[136,256]{1,0:T(8,128)S(1)}, u32[]{:S(2)}, u32[]{:S(2)}) collective-permute-start(f32[136,256]{1,0:T(8,128)S(1)} %get-tuple-element.66.refs_1_), channel_id=1, source_target_pairs={{0,6},{1,7},{2,4},{3,5},{4,2},{5,3},{6,0},{7,1},{8,14},{9,15},{10,... | collective-permute-start | bytes 417800 | tf_op jit(solution)/shard_map/ppermute | solution.py:448
  10.9 1.6 %shard_map.87 = (f32[256,256]{1,0:T(8,128)S(1)}, f32[2,256,256]{2,1,0:T(8,128)S(1)}, f32[128,256]{1,0:T(8,128)S(1)}, f32[128,256]{1,0:T(8,128)S(1)}) custom-call(s32[1]{0:T(128)} %bitcast.refs_0_, f32[2,512,256]{2,1,0:T(8,128)S(1)} %get-tuple-element.53.refs_1_, bf16[2,256,512]{2,1,0:T(8,128)(2,1)S(1)} %get-tuple-element.54.refs_2_, ...), custom_call_target="tpu_custom_call" | custom-call | flops 1 | bytes 1 | tf_op jit(solution)/shard_map/pallas_call | solution.py:475
  15.0 2.2 %collective-permute-done.10.refs_3_ = f32[136,256]{1,0:T(8,128)S(1)} collective-permute-done((f32[136,256]{1,0:T(8,128)S(1)}, f32[136,256]{1,0:T(8,128)S(1)}, u32[]{:S(2)}, u32[]{:S(2)}) %collective-permute-start.10) | collective-permute-done | bytes 139296 | tf_op jit(solution)/shard_map/ppermute | solution.py:448
  17.6 1.6 %collective-permute-start.8 = (f32[136,256]{1,0:T(8,128)S(1)}, f32[136,256]{1,0:T(8,128)S(1)}, u32[]{:S(2)}, u32[]{:S(2)}) collective-permute-start(f32[136,256]{1,0:T(8,128)S(1)} %get-tuple-element.65), channel_id=1, source_target_pairs={{0,6},{1,7},{2,4},{3,5},{4,2},{5,3},{6,0},{7,1},{8,14},{9,15},{10,... | collective-permute-start | bytes 417800 | tf_op jit(solution)/shard_map/ppermute | solution.py:448
  19.2 1.4 %collective-permute-start.6 = (f32[128,256]{1,0:T(8,128)S(1)}, f32[128,256]{1,0:T(8,128)S(1)}, u32[]{:S(2)}, u32[]{:S(2)}) collective-permute-start(f32[128,256]{1,0:T(8,128)S(1)} %get-tuple-element.63), channel_id=1, source_target_pairs={{0,2},{1,3},{2,0},{3,1},{4,6},{5,7},{6,4},{7,5},{8,10},{9,11},{10,... | collective-permute-start | bytes 393224 | tf_op jit(solution)/shard_map/ppermute | solution.py:448
  21.2 1.6 %collective-permute-start.14 = (f32[136,256]{1,0:T(8,128)S(1)}, f32[136,256]{1,0:T(8,128)S(1)}, u32[]{:S(2)}, u32[]{:S(2)}) collective-permute-start(f32[136,256]{1,0:T(8,128)S(1)} %get-tuple-element.73.refs_1_), channel_id=1, source_target_pairs={{0,8},{1,9},{2,10},{3,11},{4,12},{5,13},{6,14},{7,15},{8,0},{9,1},... | collective-permute-start | bytes 417800 | tf_op jit(solution)/shard_map/ppermute | solution.py:448
  22.8 2.6 %collective-permute-start.23 = (f32[128,256]{1,0:T(8,128)S(1)}, f32[128,256]{1,0:T(8,128)S(1)}, u32[]{:S(2)}, u32[]{:S(2)}) collective-permute-start(f32[128,256]{1,0:T(8,128)S(1)} %get-tuple-element.92.refs_1_), channel_id=1, source_target_pairs={{0,16},{1,17},{2,18},{3,19},{4,20},{5,21},{6,22},{7,23},{8,24},{9,... | collective-permute-start | bytes 393224 | tf_op jit(solution)/shard_map/ppermute | solution.py:448
  26.2 1.2 %collective-permute-done.6.refs_2_ = f32[128,256]{1,0:T(8,128)S(1)} collective-permute-done((f32[128,256]{1,0:T(8,128)S(1)}, f32[128,256]{1,0:T(8,128)S(1)}, u32[]{:S(2)}, u32[]{:S(2)}) %collective-permute-start.6) | collective-permute-done | bytes 131104 | tf_op jit(solution)/shard_map/ppermute | solution.py:448
  27.4 1.2 %shard_map.92 = (f32[128,256]{1,0:T(8,128)S(1)}, f32[152,256]{1,0:T(8,128)S(1)}, f32[4,128,256]{2,1,0:T(8,128)S(1)}) custom-call(s32[1]{0:T(128)} %bitcast.refs_0_, f32[128,256]{1,0:T(8,128)S(1)} %get-tuple-element.62.refs_5_.refs_1_, f32[128,256]{1,0:T(8,128)S(1)} %collective-permute-done.6.refs_2_, f32[128,256]{1,0:T(8,128)S(1)} %collective-permute-done.7.refs_3_, ...), custom_call_target="tpu_custom_call" | custom-call | flops 1 | bytes 1 | tf_op jit(solution)/shard_map/pallas_call | solution.py:475
  28.6 1.6 %collective-permute-start.13 = (f32[152,256]{1,0:T(8,128)S(1)}, f32[152,256]{1,0:T(8,128)S(1)}, u32[]{:S(2)}, u32[]{:S(2)}) collective-permute-start(f32[152,256]{1,0:T(8,128)S(1)} %get-tuple-element.71.refs_3_), channel_id=1, source_target_pairs={{0,8},{1,9},{2,10},{3,11},{4,12},{5,13},{6,14},{7,15},{8,0},{9,1},... | collective-permute-start | bytes 466952 | tf_op jit(solution)/shard_map/ppermute | solution.py:448
  30.3 1.2 %collective-permute-done.23.refs_2_ = f32[128,256]{1,0:T(8,128)S(1)} collective-permute-done((f32[128,256]{1,0:T(8,128)S(1)}, f32[128,256]{1,0:T(8,128)S(1)}, u32[]{:S(2)}, u32[]{:S(2)}) %collective-permute-start.23) | collective-permute-done | bytes 131104 | tf_op jit(solution)/shard_map/ppermute | solution.py:448
  31.4 1.6 %collective-permute-start.24 = (f32[128,256]{1,0:T(8,128)S(1)}, f32[128,256]{1,0:T(8,128)S(1)}, u32[]{:S(2)}, u32[]{:S(2)}) collective-permute-start(f32[128,256]{1,0:T(8,128)S(1)} %shard_map.100.refs_1_), channel_id=1, source_target_pairs={{0,2},{1,3},{2,0},{3,1},{4,6},{5,7},{6,4},{7,5},{8,10},{9,11},{10,... | collective-permute-start | bytes 393224 | tf_op jit(solution)/shard_map/ppermute | solution.py:448
  33.0 1.5 %collective-permute-start.17 = (f32[72,256]{1,0:T(8,128)S(1)}, f32[72,256]{1,0:T(8,128)S(1)}, u32[]{:S(2)}, u32[]{:S(2)}) collective-permute-start(f32[72,256]{1,0:T(8,128)S(1)} %shard_map.95), channel_id=1, source_target_pairs={{0,16},{1,17},{2,18},{3,19},{4,20},{5,21},{6,22},{7,23},{8,24},{9,... | collective-permute-start | bytes 221192 | tf_op jit(solution)/shard_map/ppermute | solution.py:448
  35.3 3.4 %collective-permute-start.16 = (f32[128,256]{1,0:T(8,128)S(1)}, f32[128,256]{1,0:T(8,128)S(1)}, u32[]{:S(2)}, u32[]{:S(2)}) collective-permute-start(f32[128,256]{1,0:T(8,128)S(1)} %get-tuple-element.77.refs_3_), channel_id=1, source_target_pairs={{0,16},{1,17},{2,18},{3,19},{4,20},{5,21},{6,22},{7,23},{8,24},{9,... | collective-permute-start | bytes 393224 | tf_op jit(solution)/shard_map/ppermute | solution.py:448
  38.7 1.5 %collective-permute-start.25 = (f32[128,256]{1,0:T(8,128)S(1)}, f32[128,256]{1,0:T(8,128)S(1)}, u32[]{:S(2)}, u32[]{:S(2)}) collective-permute-start(f32[128,256]{1,0:T(8,128)S(1)} %shard_map.101.refs_1_), channel_id=1, source_target_pairs={{0,4},{1,5},{2,6},{3,7},{4,0},{5,1},{6,2},{7,3},{8,12},{9,13},{10,... | collective-permute-start | bytes 393224 | tf_op jit(solution)/shard_map/ppermute | solution.py:448
  40.6 1.3 %collective-permute-done.18.refs_3_ = f32[72,256]{1,0:T(8,128)S(1)} collective-permute-done((f32[72,256]{1,0:T(8,128)S(1)}, f32[72,256]{1,0:T(8,128)S(1)}, u32[]{:S(2)}, u32[]{:S(2)}) %collective-permute-start.18) | collective-permute-done | bytes 73760 | tf_op jit(solution)/shard_map/ppermute | solution.py:448
  42.0 1.1 %shard_map.97 = (f32[8,256]{1,0:T(8,128)S(1)}, f32[512,1024]{1,0:T(8,128)}, f32[512,256]{1,0:T(8,128)}) custom-call(s32[1]{0:T(128)} %bitcast.refs_0_, f32[2,256,256]{2,1,0:T(8,128)S(1)} %get-tuple-element.80.refs_1_, f32[2,256,256]{2,1,0:T(8,128)S(1)} %get-tuple-element.81.refs_2_, f32[256,256]{1,0:T(8,128)S(1)} %get-tuple-element.82.refs_3_.refs_13_, ...), custom_call_target="tpu_custom_call" | custom-call | flops 1 | bytes 1 | tf_op jit(solution)/shard_map/pallas_call | solution.py:475
  43.1 1.5 %collective-permute-done.16.refs_4_ = f32[128,256]{1,0:T(8,128)S(1)} collective-permute-done((f32[128,256]{1,0:T(8,128)S(1)}, f32[128,256]{1,0:T(8,128)S(1)}, u32[]{:S(2)}, u32[]{:S(2)}) %collective-permute-start.16) | collective-permute-done | bytes 131104 | tf_op jit(solution)/shard_map/ppermute | solution.py:448
  45.3 1.5 %collective-permute-start.21 = (f32[168,256]{1,0:T(8,128)S(1)}, f32[168,256]{1,0:T(8,128)S(1)}, u32[]{:S(2)}, u32[]{:S(2)}) collective-permute-start(f32[168,256]{1,0:T(8,128)S(1)} %get-tuple-element.87), channel_id=1, source_target_pairs={{0,6},{1,7},{2,4},{3,5},{4,2},{5,3},{6,0},{7,1},{8,14},{9,15},{10,... | collective-permute-start | bytes 516104 | tf_op jit(solution)/shard_map/ppermute | solution.py:448
  46.9 1.0 %collective-permute-start.19 = (f32[160,256]{1,0:T(8,128)S(1)}, f32[160,256]{1,0:T(8,128)S(1)}, u32[]{:S(2)}, u32[]{:S(2)}) collective-permute-start(f32[160,256]{1,0:T(8,128)S(1)} %get-tuple-element.85), channel_id=1, source_target_pairs={{0,2},{1,3},{2,0},{3,1},{4,6},{5,7},{6,4},{7,5},{8,10},{9,11},{10,... | collective-permute-start | bytes 491528 | tf_op jit(solution)/shard_map/ppermute | solution.py:448
  49.0 5.0 %collective-permute-done.26.refs_2_ = f32[128,256]{1,0:T(8,128)S(1)} collective-permute-done((f32[128,256]{1,0:T(8,128)S(1)}, f32[128,256]{1,0:T(8,128)S(1)}, u32[]{:S(2)}, u32[]{:S(2)}) %collective-permute-start.26) | collective-permute-done | bytes 131104 | tf_op jit(solution)/shard_map/ppermute | solution.py:448
  54.0 1.3 %collective-permute-done.19.refs_2_ = f32[160,256]{1,0:T(8,128)S(1)} collective-permute-done((f32[160,256]{1,0:T(8,128)S(1)}, f32[160,256]{1,0:T(8,128)S(1)}, u32[]{:S(2)}, u32[]{:S(2)}) %collective-permute-start.19) | collective-permute-done | bytes 163872 | tf_op jit(solution)/shard_map/ppermute | solution.py:448
  57.9 1.5 %shard_map.106 = (f32[512,1024]{1,0:T(8,128)}, f32[512,256]{1,0:T(8,128)}, f32[256,256]{1,0:T(8,128)}) custom-call(s32[1]{0:T(128)} %bitcast.refs_0_, f32[160,256]{1,0:T(8,128)S(1)} %get-tuple-element.84.refs_1_.refs_5_, f32[160,256]{1,0:T(8,128)S(1)} %collective-permute-done.19.refs_2_, ...), custom_call_target="tpu_custom_call", output_to_operand_aliasing={{0}: (14, {}), {1}: (15, {})} | custom-call | flops 1 | bytes 1 | tf_op jit(solution)/shard_map/pallas_call | solution.py:475
  (60 shorter events, 12.3 us)
Async XLA Ops:
  0.7 5.4 %collective-permute-start.2 = (f32[256,256]{1,0:T(8,128)}, f32[256,256]{1,0:T(8,128)S(1)}, u32[]{:S(2)}, u32[]{:S(2)}) collective-permute-start(f32[256,256]{1,0:T(8,128)} %refs_1_.3), channel_id=1, source_target_pairs={{0,1},{1,0},{2,3},{3,2},{4,5},{5,4},{6,7},{7,6},{8,9},{9,8},{10,11... | collective-permute-start | bytes 786440 | tf_op jit(solution)/shard_map/ppermute | solution.py:448
  1.2 4.8 %collective-permute-start.3 = (f32[256,256]{1,0:T(8,128)}, f32[256,256]{1,0:T(8,128)S(1)}, u32[]{:S(2)}, u32[]{:S(2)}) collective-permute-start(f32[256,256]{1,0:T(8,128)} %refs_2_.3), channel_id=1, source_target_pairs={{0,1},{1,0},{2,3},{3,2},{4,5},{5,4},{6,7},{7,6},{8,9},{9,8},{10,11... | collective-permute-start | bytes 786440 | tf_op jit(solution)/shard_map/ppermute | solution.py:448
  5.4 5.5 %collective-permute-start = (f32[192,256]{1,0:T(8,128)S(1)}, f32[192,256]{1,0:T(8,128)S(1)}, u32[]{:S(2)}, u32[]{:S(2)}) collective-permute-start(f32[192,256]{1,0:T(8,128)S(1)} %get-tuple-element.50), channel_id=1, source_target_pairs={{0,1},{1,0},{2,3},{3,2},{4,5},{5,4},{6,7},{7,6},{8,9},{9,8},{10,11... | collective-permute-start | bytes 589832 | tf_op jit(solution)/shard_map/ppermute | solution.py:448
  5.9 5.0 %collective-permute-start.1 = (f32[192,256]{1,0:T(8,128)S(1)}, f32[192,256]{1,0:T(8,128)S(1)}, u32[]{:S(2)}, u32[]{:S(2)}) collective-permute-start(f32[192,256]{1,0:T(8,128)S(1)} %get-tuple-element.51), channel_id=1, source_target_pairs={{0,1},{1,0},{2,3},{3,2},{4,5},{5,4},{6,7},{7,6},{8,9},{9,8},{10,11... | collective-permute-start | bytes 589832 | tf_op jit(solution)/shard_map/ppermute | solution.py:448
  6.4 8.7 %collective-permute-start.11 = (f32[136,256]{1,0:T(8,128)S(1)}, f32[136,256]{1,0:T(8,128)S(1)}, u32[]{:S(2)}, u32[]{:S(2)}) collective-permute-start(f32[136,256]{1,0:T(8,128)S(1)} %get-tuple-element.66.refs_1_), channel_id=1, source_target_pairs={{0,6},{1,7},{2,4},{3,5},{4,2},{5,3},{6,0},{7,1},{8,14},{9,15},{10,... | collective-permute-start | bytes 417800 | tf_op jit(solution)/shard_map/ppermute | solution.py:448
  10.3 6.9 %collective-permute-start.10 = (f32[136,256]{1,0:T(8,128)S(1)}, f32[136,256]{1,0:T(8,128)S(1)}, u32[]{:S(2)}, u32[]{:S(2)}) collective-permute-start(f32[136,256]{1,0:T(8,128)S(1)} %get-tuple-element.66.refs_1_), channel_id=1, source_target_pairs={{0,4},{1,5},{2,6},{3,7},{4,0},{5,1},{6,2},{7,3},{8,12},{9,13},{10,... | collective-permute-start | bytes 417800 | tf_op jit(solution)/shard_map/ppermute | solution.py:448
  10.8 6.7 %collective-permute-start.9 = (f32[136,256]{1,0:T(8,128)S(1)}, f32[136,256]{1,0:T(8,128)S(1)}, u32[]{:S(2)}, u32[]{:S(2)}) collective-permute-start(f32[136,256]{1,0:T(8,128)S(1)} %get-tuple-element.66.refs_1_), channel_id=1, source_target_pairs={{0,2},{1,3},{2,0},{3,1},{4,6},{5,7},{6,4},{7,5},{8,10},{9,11},{10,... | collective-permute-start | bytes 417800 | tf_op jit(solution)/shard_map/ppermute | solution.py:448
  17.6 5.2 %collective-permute-start.12 = (f32[3,136,256]{2,1,0:T(8,128)S(1)}, f32[3,136,256]{2,1,0:T(8,128)S(1)}, u32[]{:S(2)}, u32[]{:S(2)}) collective-permute-start(f32[3,136,256]{2,1,0:T(8,128)S(1)} %get-tuple-element.67.refs_2_.refs_4_), channel_id=1, source_target_pairs={{0,1},{1,0},{2,3},{3,2},{4,5},{5,4},{6,7},{7,6},{8,9},{9,8},{10,11... | collective-permute-start | bytes 1253384 | tf_op jit(solution)/shard_map/ppermute | solution.py:448
  17.6 9.8 %collective-permute-start.8 = (f32[136,256]{1,0:T(8,128)S(1)}, f32[136,256]{1,0:T(8,128)S(1)}, u32[]{:S(2)}, u32[]{:S(2)}) collective-permute-start(f32[136,256]{1,0:T(8,128)S(1)} %get-tuple-element.65), channel_id=1, source_target_pairs={{0,6},{1,7},{2,4},{3,5},{4,2},{5,3},{6,0},{7,1},{8,14},{9,15},{10,... | collective-permute-start | bytes 417800 | tf_op jit(solution)/shard_map/ppermute | solution.py:448
  19.2 8.2 %collective-permute-start.6 = (f32[128,256]{1,0:T(8,128)S(1)}, f32[128,256]{1,0:T(8,128)S(1)}, u32[]{:S(2)}, u32[]{:S(2)}) collective-permute-start(f32[128,256]{1,0:T(8,128)S(1)} %get-tuple-element.63), channel_id=1, source_target_pairs={{0,2},{1,3},{2,0},{3,1},{4,6},{5,7},{6,4},{7,5},{8,10},{9,11},{10,... | collective-permute-start | bytes 393224 | tf_op jit(solution)/shard_map/ppermute | solution.py:448
  20.6 6.9 %collective-permute-start.7 = (f32[128,256]{1,0:T(8,128)S(1)}, f32[128,256]{1,0:T(8,128)S(1)}, u32[]{:S(2)}, u32[]{:S(2)}) collective-permute-start(f32[128,256]{1,0:T(8,128)S(1)} %get-tuple-element.64), channel_id=1, source_target_pairs={{0,4},{1,5},{2,6},{3,7},{4,0},{5,1},{6,2},{7,3},{8,12},{9,13},{10,... | collective-permute-start | bytes 393224 | tf_op jit(solution)/shard_map/ppermute | solution.py:448
  21.2 9.1 %collective-permute-start.14 = (f32[136,256]{1,0:T(8,128)S(1)}, f32[136,256]{1,0:T(8,128)S(1)}, u32[]{:S(2)}, u32[]{:S(2)}) collective-permute-start(f32[136,256]{1,0:T(8,128)S(1)} %get-tuple-element.73.refs_1_), channel_id=1, source_target_pairs={{0,8},{1,9},{2,10},{3,11},{4,12},{5,13},{6,14},{7,15},{8,0},{9,1},... | collective-permute-start | bytes 417800 | tf_op jit(solution)/shard_map/ppermute | solution.py:448
  22.8 8.7 %collective-permute-start.23 = (f32[128,256]{1,0:T(8,128)S(1)}, f32[128,256]{1,0:T(8,128)S(1)}, u32[]{:S(2)}, u32[]{:S(2)}) collective-permute-start(f32[128,256]{1,0:T(8,128)S(1)} %get-tuple-element.92.refs_1_), channel_id=1, source_target_pairs={{0,16},{1,17},{2,18},{3,19},{4,20},{5,21},{6,22},{7,23},{8,24},{9,... | collective-permute-start | bytes 393224 | tf_op jit(solution)/shard_map/ppermute | solution.py:448
  28.6 6.1 %collective-permute-start.13 = (f32[152,256]{1,0:T(8,128)S(1)}, f32[152,256]{1,0:T(8,128)S(1)}, u32[]{:S(2)}, u32[]{:S(2)}) collective-permute-start(f32[152,256]{1,0:T(8,128)S(1)} %get-tuple-element.71.refs_3_), channel_id=1, source_target_pairs={{0,8},{1,9},{2,10},{3,11},{4,12},{5,13},{6,14},{7,15},{8,0},{9,1},... | collective-permute-start | bytes 466952 | tf_op jit(solution)/shard_map/ppermute | solution.py:448
  30.3 4.3 %collective-permute-start.15 = (f32[136,256]{1,0:T(8,128)S(1)}, f32[136,256]{1,0:T(8,128)S(1)}, u32[]{:S(2)}, u32[]{:S(2)}) collective-permute-start(f32[136,256]{1,0:T(8,128)S(1)} %collective-permute-done.14.refs_2_), channel_id=1, source_target_pairs={{0,1},{1,0},{2,3},{3,2},{4,5},{5,4},{6,7},{7,6},{8,9},{9,8},{10,11... | collective-permute-start | bytes 417800 | tf_op jit(solution)/shard_map/ppermute | solution.py:448
  31.4 7.2 %collective-permute-start.24 = (f32[128,256]{1,0:T(8,128)S(1)}, f32[128,256]{1,0:T(8,128)S(1)}, u32[]{:S(2)}, u32[]{:S(2)}) collective-permute-start(f32[128,256]{1,0:T(8,128)S(1)} %shard_map.100.refs_1_), channel_id=1, source_target_pairs={{0,2},{1,3},{2,0},{3,1},{4,6},{5,7},{6,4},{7,5},{8,10},{9,11},{10,... | collective-permute-start | bytes 393224 | tf_op jit(solution)/shard_map/ppermute | solution.py:448
  33.0 7.6 %collective-permute-start.17 = (f32[72,256]{1,0:T(8,128)S(1)}, f32[72,256]{1,0:T(8,128)S(1)}, u32[]{:S(2)}, u32[]{:S(2)}) collective-permute-start(f32[72,256]{1,0:T(8,128)S(1)} %shard_map.95), channel_id=1, source_target_pairs={{0,16},{1,17},{2,18},{3,19},{4,20},{5,21},{6,22},{7,23},{8,24},{9,... | collective-permute-start | bytes 221192 | tf_op jit(solution)/shard_map/ppermute | solution.py:448
  35.3 9.3 %collective-permute-start.16 = (f32[128,256]{1,0:T(8,128)S(1)}, f32[128,256]{1,0:T(8,128)S(1)}, u32[]{:S(2)}, u32[]{:S(2)}) collective-permute-start(f32[128,256]{1,0:T(8,128)S(1)} %get-tuple-element.77.refs_3_), channel_id=1, source_target_pairs={{0,16},{1,17},{2,18},{3,19},{4,20},{5,21},{6,22},{7,23},{8,24},{9,... | collective-permute-start | bytes 393224 | tf_op jit(solution)/shard_map/ppermute | solution.py:448
  38.7 10.2 %collective-permute-start.25 = (f32[128,256]{1,0:T(8,128)S(1)}, f32[128,256]{1,0:T(8,128)S(1)}, u32[]{:S(2)}, u32[]{:S(2)}) collective-permute-start(f32[128,256]{1,0:T(8,128)S(1)} %shard_map.101.refs_1_), channel_id=1, source_target_pairs={{0,4},{1,5},{2,6},{3,7},{4,0},{5,1},{6,2},{7,3},{8,12},{9,13},{10,... | collective-permute-start | bytes 393224 | tf_op jit(solution)/shard_map/ppermute | solution.py:448
  45.3 10.7 %collective-permute-start.21 = (f32[168,256]{1,0:T(8,128)S(1)}, f32[168,256]{1,0:T(8,128)S(1)}, u32[]{:S(2)}, u32[]{:S(2)}) collective-permute-start(f32[168,256]{1,0:T(8,128)S(1)} %get-tuple-element.87), channel_id=1, source_target_pairs={{0,6},{1,7},{2,4},{3,5},{4,2},{5,3},{6,0},{7,1},{8,14},{9,15},{10,... | collective-permute-start | bytes 516104 | tf_op jit(solution)/shard_map/ppermute | solution.py:448
  46.9 8.4 %collective-permute-start.19 = (f32[160,256]{1,0:T(8,128)S(1)}, f32[160,256]{1,0:T(8,128)S(1)}, u32[]{:S(2)}, u32[]{:S(2)}) collective-permute-start(f32[160,256]{1,0:T(8,128)S(1)} %get-tuple-element.85), channel_id=1, source_target_pairs={{0,2},{1,3},{2,0},{3,1},{4,6},{5,7},{6,4},{7,5},{8,10},{9,11},{10,... | collective-permute-start | bytes 491528 | tf_op jit(solution)/shard_map/ppermute | solution.py:448
  47.9 8.1 %collective-permute-start.20 = (f32[160,256]{1,0:T(8,128)S(1)}, f32[160,256]{1,0:T(8,128)S(1)}, u32[]{:S(2)}, u32[]{:S(2)}) collective-permute-start(f32[160,256]{1,0:T(8,128)S(1)} %get-tuple-element.86), channel_id=1, source_target_pairs={{0,4},{1,5},{2,6},{3,7},{4,0},{5,1},{6,2},{7,3},{8,12},{9,13},{10,... | collective-permute-start | bytes 491528 | tf_op jit(solution)/shard_map/ppermute | solution.py:448
  48.9 5.0 %collective-permute-start.26 = (f32[128,256]{1,0:T(8,128)S(1)}, f32[128,256]{1,0:T(8,128)S(1)}, u32[]{:S(2)}, u32[]{:S(2)}) collective-permute-start(f32[128,256]{1,0:T(8,128)S(1)} %shard_map.102.refs_1_), channel_id=1, source_target_pairs={{0,8},{1,9},{2,10},{3,11},{4,12},{5,13},{6,14},{7,15},{8,0},{9,1},... | collective-permute-start | bytes 393224 | tf_op jit(solution)/shard_map/ppermute | solution.py:448
  55.3 2.6 %collective-permute-start.22 = (f32[2,160,256]{2,1,0:T(8,128)S(1)}, f32[2,160,256]{2,1,0:T(8,128)S(1)}, u32[]{:S(2)}, u32[]{:S(2)}) collective-permute-start(f32[2,160,256]{2,1,0:T(8,128)S(1)} %shard_map.99.refs_5_), channel_id=1, source_target_pairs={{0,1},{1,0},{2,3},{3,2},{4,5},{5,4},{6,7},{7,6},{8,9},{9,8},{10,11... | collective-permute-start | bytes 983048 | tf_op jit(solution)/shard_map/ppermute | solution.py:448
  (7 other events, 18.7 us)
